TPU v7x, 32 devices: a whole 2x2x4 slice. The times are simulated.
32 devices in a mesh: dp: 4 (over y, x), mp: 8 (over z, core).
Axes of the slice: x: 2, y: 2, z: 4, core: 2. Of those that a mesh axis runs over, the one named last changes fastest.
Arguments:
- activations: bfloat16 [4096, 2048], P('dp', 'mp'), may hold values from -6 to 6
- out_grad: bfloat16 [4096, 8192], P('dp'), may hold values from -0.8984375 to 0.8984375
- old_weight: bfloat16 [8, 256, 8192], P('mp', 'dp'), may hold values from -0.125 to 0.125
- old_first: float32 [8, 256, 8192], P('mp', 'dp'), may hold values from -6 to 6
- old_second: float32 [8, 256, 8192], P('mp', 'dp'), may hold values from 0.25 to 4
- step: int32 [1], replicated, may hold values from 1 to 31
- next_input: bfloat16 [4096, 2048], P('dp', 'mp'), may hold values from -6 to 6
Outputs:
- new_weight: bfloat16 [8, 344, 8192], P('mp', 'dp')
- new_first: float32 [8, 344, 8192], P('mp', 'dp')
- new_second: float32 [8, 344, 8192], P('mp', 'dp')
- output: bfloat16 [4096, 8192], P('dp', 'mp')
Inputs may be any that keep to these rules, and one draw needn't show every extreme that they name: `step`: the number of Adam steps taken, this one included.
All inputs are finite; a program needn't handle non-finite values.
Results may differ from a plain program's by a relative error of at most 0.0049.
Values may be sent and summed in bfloat16 or wider, within the bound.
A program may use at most 192 MiB of HBM per device.

v0:
```python
import jax
import jax.numpy as jnp
from jax import lax
from jax.sharding import PartitionSpec as P


def partner(i, k, n):
    return i ^ k if n & n - 1 == 0 else (i + k) % n


def exchange(block, axis, k):
    n = lax.axis_size(axis)
    return lax.ppermute(block, axis, [(i, partner(i, k, n)) for i in range(n)])


def target(k, n, axis):
    me = lax.axis_index(axis)
    return me ^ k if n & n - 1 == 0 else lax.rem(me + k, n)


def to_front(block, axis):
    n = lax.axis_size(axis)
    return lax.ppermute(block, axis, [(i, i - 1) for i in range(1, n)])


def body(activations, out_grad, old_weight, old_first, old_second, step, next_input):
    owners = lax.axis_size("dp")
    owner = lax.axis_index("dp")
    old_rows = old_weight.shape[1]
    width = old_weight.shape[2]
    held_rows = old_rows * owners
    shard_rows = (held_rows + owners - 2) // (owners - 1)
    input_all = lax.all_gather(next_input, "mp", axis=1, tiled=True)
    part = lax.dot_general(
        activations, out_grad, (((0,), (0,)), ((), ())), preferred_element_type=jnp.float32
    ).astype(jnp.bfloat16)
    part = part.reshape(owners, old_rows, width)
    grad = lax.dynamic_index_in_dim(part, owner, 0, keepdims=False).astype(jnp.float32)
    for k in range(1, owners):
        away = lax.dynamic_index_in_dim(part, target(k, owners, "dp"), 0, keepdims=False)
        grad = grad + exchange(away, "dp", k).astype(jnp.float32)
    step_float = step[0].astype(jnp.float32)
    first_fix = 1.0 - jnp.power(jnp.float32(0.9), step_float)
    second_fix = 1.0 - jnp.power(jnp.float32(0.95), step_float)
    new_first = 0.9 * old_first[0] + 0.1 * grad
    new_second = 0.95 * old_second[0] + 0.05 * grad * grad
    update = new_first / first_fix / (jnp.sqrt(new_second / second_fix) + 1e-08)
    new_weight = (old_weight[0].astype(jnp.float32) - 0.01 * update).astype(jnp.bfloat16)
    weight_part = lax.all_to_all(new_weight, "mp", split_axis=1, concat_axis=0, tiled=True)
    heads = lax.axis_size("mp")
    weight_part = weight_part.reshape(heads, old_rows, -1)
    weight_cols = lax.all_gather(weight_part, "dp", axis=1, tiled=True)
    weight_cols = weight_cols.reshape(heads * held_rows, -1)
    begin = owner * (shard_rows - old_rows)

    def mine(block):
        behind = to_front(block.astype(jnp.bfloat16), "dp").astype(block.dtype)
        rows = jnp.concatenate([block, behind, jnp.zeros((shard_rows, width), block.dtype)], 0)
        return lax.dynamic_slice_in_dim(rows, begin, shard_rows, 0)[None]

    outs = (mine(new_weight), mine(new_first), mine(new_second))
    output = jnp.dot(input_all, weight_cols, preferred_element_type=jnp.float32).astype(
        jnp.bfloat16
    )
    return (*outs, output)


def solution(mesh):
    return jax.shard_map(
        body,
        mesh=mesh,
        in_specs=(
            P("dp", "mp"),
            P("dp", None),
            P("mp", "dp", None),
            P("mp", "dp", None),
            P("mp", "dp", None),
            P(),
            P("dp", "mp"),
        ),
        out_specs=(P("mp", "dp", None), P("mp", "dp", None), P("mp", "dp", None), P("dp", "mp")),
        check_vma=False,
    )
```

profile of v0, /device:TPU:0, one launch (start us, length us, event | category | flops | bytes accessed | tf_op | source)
XLA Modules:
  0.0 292.9 jit_solution(17170010049314651664)
XLA Ops:
  7.2 0.0 copy-start
  7.2 0.0 all-gather.3.cloned.1.call-start
  7.2 1.0 copy-done
  8.2 10.7 %convolution_convert_fusion = bf16[256,8192]{1,0:T(8,128)(2,1)S(1)} fusion(bf16[1024,256]{1,0:T(8,128)(2,1)S(1)} %copy-done, bf16[1024,8192]{1,0:T(8,128)(2,1)} %param.8), kind=kOutput, calls=%fused_computation | convolution fusion | flops 4297064448 | bytes 21495808 | tf_op jit(solution)/shard_map/dot_general | solution.py:34
  19.0 0.0 copy-start.4
  19.0 1.8 dynamic-slice_bitcast_fusion.2
  20.7 1.2 copy-done.4
  21.9 2.9 %collective-permute-start = (bf16[64,8192]{1,0:T(8,128)(2,1)}, bf16[64,8192]{1,0:T(8,128)(2,1)S(1)}, u32[]{:S(2)}, u32[]{:S(2)}) collective-permute-start(bf16[64,8192]{1,0:T(8,128)(2,1)} %get-tuple-element.26), channel_id=1, source_target_pairs={{0,8},{8,0},{16,24},{24,16},{1,9},{9,1},{17,25},{25,17},{2,10},{10... | collective-permute-start | bytes 3145736 | tf_op jit(solution)/shard_map/ppermute | solution.py:13
  24.8 1.5 collective-permute-start.1
  26.4 0.0 collective-permute-start.2
  27.1 0.0 copy-start.9
  27.1 21.9 %collective-permute-done = bf16[64,8192]{1,0:T(8,128)(2,1)S(1)} collective-permute-done((bf16[64,8192]{1,0:T(8,128)(2,1)}, bf16[64,8192]{1,0:T(8,128)(2,1)S(1)}, u32[]{:S(2)}, u32[]{:S(2)}) %collective-permute-start) | collective-permute-done | bytes 1048608 | tf_op jit(solution)/shard_map/ppermute | solution.py:13
  49.0 0.0 copy-start.7
  49.0 23.1 %collective-permute-done.1 = bf16[64,8192]{1,0:T(8,128)(2,1)S(1)} collective-permute-done((bf16[64,8192]{1,0:T(8,128)(2,1)}, bf16[64,8192]{1,0:T(8,128)(2,1)S(1)}, u32[]{:S(2)}, u32[]{:S(2)}) %collective-permute-start.1) | collective-permute-done | bytes 1048608 | tf_op jit(solution)/shard_map/ppermute | solution.py:13
  72.1 0.0 copy-done.7
  72.2 0.0 copy-start.8
  72.2 1.0 copy-done.8
  73.1 0.0 collective-permute-done.2
  73.1 5.9 %fusion.11 = (bf16[64,8192]{1,0:T(8,128)(2,1)}, f32[64,8192]{1,0:T(8,128)S(1)}, bf16[64,8192]{1,0:T(8,128)(2,1)}, f32[64,8192]{1,0:T(8,128)S(1)}) fusion(bf16[64,8192]{1,0:T(8,128)(2,1)} %collective-permute-done.2, bf16[64,8192]{1,0:T(8,128)(2,1)} %copy-done.8, bf16[64,8192]{1,0:T(8,128)(2,1)} %copy-done.7, bf16[4,64,8192]{2,1,0:T(8,128)(2,1)} %bitcast.42, ...), kind=kLoop, calls=%fused_computation.29 | loop fusion | flops 8388608 | bytes 14680068 | tf_op jit(solution)/shard_map/convert_element_type | solution.py:57
  79.0 0.0 copy-start.2
  79.0 0.0 copy-done.9
  79.0 1.1 fusion.7
  80.1 0.2 copy-done.2
  80.3 0.0 copy-start.6
  80.3 0.1 copy.21
  80.4 31.3 %all_to_all.16 = bf16[64,8,1024]{2,0,1:T(8,128)(2,1)S(1)} all-to-all(bf16[64,8,1024]{2,0,1:T(8,128)(2,1)S(1)} %bitcast.46), channel_id=1, replica_groups=mesh['dp'=4,'mp'=8] {'mp'}, dimensions={1} | all-to-all | bytes 2097152 | tf_op jit(solution)/shard_map/all_to_all | solution.py:49
  111.7 0.0 copy-done.6
  111.7 1.5 copy.16
  113.2 0.0 all-gather.3.cloned.1.call-update
  113.2 0.0 all-gather.5.cloned.1.call-start
  113.3 0.7 all-gather.5.cloned.1.call-update
  114.0 1.3 collective-permute-start.4
  115.3 1.3 collective-permute-start.5
  116.6 0.1 pad_dynamic-slice_fusion.6
  116.7 0.1 pad_dynamic-slice_fusion.7
  116.8 1.5 collective-permute-start.3
  118.2 35.3 %collective-permute-done.4 = bf16[64,8192]{1,0:T(8,128)(2,1)} collective-permute-done((bf16[64,8192]{1,0:T(8,128)(2,1)}, bf16[64,8192]{1,0:T(8,128)(2,1)}, u32[]{:S(2)}, u32[]{:S(2)}) %collective-permute-start.4) | collective-permute-done | bytes 1048608 | tf_op jit(solution)/shard_map/ppermute | solution.py:23
  153.5 1.4 convert_element_type.60
  154.9 0.0 copy-start.3
  154.9 21.1 %collective-permute-done.5 = bf16[64,8192]{1,0:T(8,128)(2,1)} collective-permute-done((bf16[64,8192]{1,0:T(8,128)(2,1)}, bf16[64,8192]{1,0:T(8,128)(2,1)}, u32[]{:S(2)}, u32[]{:S(2)}) %collective-permute-start.5) | collective-permute-done | bytes 1048608 | tf_op jit(solution)/shard_map/ppermute | solution.py:23
  176.0 1.4 convert_element_type.62
  177.4 0.0 copy-done.3
  177.4 4.0 %fusion.1 = (f32[86,8192]{1,0:T(8,128)}, f32[86,8192]{1,0:T(8,128)}) fusion(s32[]{:T(128)S(6)} %select_n.22, f32[64,8192]{1,0:T(8,128)S(1)} %get-tuple-element.21, f32[64,8192]{1,0:T(8,128)S(1)} %convert_element_type.62, f32[86]{0:T(128)S(1)} %pad_dynamic-slice_fusion.6, f32[64,8192]{1,0:T(8,128)S(1)} %convert_element_type.60, f32[64,8192]{1,0:T(8,128)S(1)} %copy-done.3), kind=kLoop, calls=%fused_computation.9 | loop fusion | flops 2818048 | bytes 14025052 | tf_op jit(solution)/shard_map/concatenate | solution.py:58
  181.3 0.0 copy-start.5
  181.3 6.7 %broadcast_in_dim.14 = f32[1,86,8192]{2,0,1:T(1,128)} reshape(f32[86,8192]{1,0:T(8,128)} %get-tuple-element.30) | data formatting | bytes 5636096 | tf_op jit(solution)/shard_map/broadcast_in_dim | solution.py:59
  188.0 0.0 copy-done.5
  188.0 4.7 %broadcast_in_dim.15 = f32[1,86,8192]{2,0,1:T(1,128)} reshape(f32[86,8192]{1,0:T(8,128)S(1)} %copy-done.5) | data formatting | bytes 5636096 | tf_op jit(solution)/shard_map/broadcast_in_dim | solution.py:59
  192.8 4.1 %collective-permute-done.3 = bf16[64,8192]{1,0:T(8,128)(2,1)} collective-permute-done((bf16[64,8192]{1,0:T(8,128)(2,1)}, bf16[64,8192]{1,0:T(8,128)(2,1)}, u32[]{:S(2)}, u32[]{:S(2)}) %collective-permute-start.3) | collective-permute-done | bytes 1048608 | tf_op jit(solution)/shard_map/ppermute | solution.py:23
  196.9 3.4 %fusion.10 = bf16[1,86,8192]{2,1,0:T(8,128)(2,1)} fusion(s32[]{:T(128)S(6)} %select_n.22, bf16[64,8192]{1,0:T(8,128)(2,1)} %copy-done.6, bf16[64,8192]{1,0:T(8,128)(2,1)} %collective-permute-done.3, bf16[86]{0:T(256)(128)(2,1)S(1)} %pad_dynamic-slice_fusion.7), kind=kLoop, calls=%fused_computation.22 | loop fusion | flops 4227072 | bytes 3506352 | tf_op jit(solution)/shard_map/broadcast_in_dim | solution.py:59
  200.3 25.5 %all-gather.3.cloned.1.call-done = bf16[8,256,1024]{2,0,1:T(8,128)(2,1)} async-done(((bf16[8,64,1024]{2,0,1:T(8,128)(2,1)}), bf16[8,256,1024]{2,0,1:T(8,128)(2,1)}) %all-gather.3.cloned.1.call-update) | async-done | bytes 4194320 | tf_op jit(solution)/shard_map/all_gather | solution.py:52
  225.8 6.5 %copy.17 = bf16[8,256,1024]{2,1,0:T(8,128)(2,1)} copy(bf16[8,256,1024]{2,0,1:T(8,128)(2,1)} %all-gather.3.cloned.1.call-done) | data formatting | bytes 8388608 | tf_op jit(solution)/shard_map/all_gather | solution.py:52
  232.3 42.9 %all-gather.5.cloned.1.call-done = bf16[1024,2048]{1,0:T(8,128)(2,1)} async-done(((bf16[1024,256]{1,0:T(8,128)(2,1)}), bf16[1024,2048]{1,0:T(8,128)(2,1)}) %all-gather.5.cloned.1.call-update) | async-done | bytes 4194320 | tf_op jit(solution)/shard_map/all_gather | solution.py:33
  275.2 0.0 copy-start.1
  275.2 8.3 %convert_bitcast_fusion = bf16[1024,1024]{0,1:T(8,128)(2,1)S(1)} fusion(bf16[2048,1024]{1,0:T(8,128)(2,1)} %bitcast.44, bf16[1024,2048]{1,0:T(8,128)(2,1)} %all-gather.5.cloned.1.call-done), kind=kOutput, calls=%fused_computation.19 | convolution fusion | flops 4296015872 | bytes 10485760 | tf_op jit(solution)/shard_map/dot_general | solution.py:62
  283.5 2.6 copy.18
  286.0 0.0 copy-done.1
  (2 shorter events, 0.0 us)
Async XLA Ops:
  7.2 1.1 copy-start
  7.2 218.6 %all-gather.3.cloned.1.call-start = ((), (), s32[]{:S(2)}) async-start(), calls=%async_computation.1 | async-start | bytes 5242880 | tf_op jit(solution)/shard_map/all_gather | solution.py:52
  19.0 2.9 %copy-start.4 = (bf16[256,8192]{1,0:T(8,128)(2,1)}, bf16[256,8192]{1,0:T(8,128)(2,1)S(1)}, u32[]{:S(2)}) copy-start(bf16[256,8192]{1,0:T(8,128)(2,1)S(1)} %convolution_convert_fusion) | copy-start | bytes 12582916
  21.9 27.1 %collective-permute-start = (bf16[64,8192]{1,0:T(8,128)(2,1)}, bf16[64,8192]{1,0:T(8,128)(2,1)S(1)}, u32[]{:S(2)}, u32[]{:S(2)}) collective-permute-start(bf16[64,8192]{1,0:T(8,128)(2,1)} %get-tuple-element.26), channel_id=1, source_target_pairs={{0,8},{8,0},{16,24},{24,16},{1,9},{9,1},{17,25},{25,17},{2,10},{10... | collective-permute-start | bytes 3145736 | tf_op jit(solution)/shard_map/ppermute | solution.py:13
  24.8 47.3 %collective-permute-start.1 = (bf16[64,8192]{1,0:T(8,128)(2,1)}, bf16[64,8192]{1,0:T(8,128)(2,1)S(1)}, u32[]{:S(2)}, u32[]{:S(2)}) collective-permute-start(bf16[64,8192]{1,0:T(8,128)(2,1)} %get-tuple-element.28), channel_id=1, source_target_pairs={{0,16},{8,24},{16,0},{24,8},{1,17},{9,25},{17,1},{25,9},{2,18},{10... | collective-permute-start | bytes 3145736 | tf_op jit(solution)/shard_map/ppermute | solution.py:13
  26.4 46.8 %collective-permute-start.2 = (bf16[64,8192]{1,0:T(8,128)(2,1)}, bf16[64,8192]{1,0:T(8,128)(2,1)}, u32[]{:S(2)}, u32[]{:S(2)}) collective-permute-start(bf16[64,8192]{1,0:T(8,128)(2,1)} %get-tuple-element.27), channel_id=1, source_target_pairs={{0,24},{8,16},{16,8},{24,0},{1,25},{9,17},{17,9},{25,1},{2,26},{10... | collective-permute-start | bytes 3145736 | tf_op jit(solution)/shard_map/ppermute | solution.py:13
  27.1 51.9 %copy-start.9 = (bf16[1,64,8192]{2,1,0:T(8,128)(2,1)S(1)}, bf16[1,64,8192]{2,1,0:T(8,128)(2,1)}, u32[]{:S(2)}) copy-start(bf16[1,64,8192]{2,1,0:T(8,128)(2,1)} %param.9) | copy-start | bytes 3145732
  49.0 23.1 %copy-start.7 = (bf16[64,8192]{1,0:T(8,128)(2,1)}, bf16[64,8192]{1,0:T(8,128)(2,1)S(1)}, u32[]{:S(2)}) copy-start(bf16[64,8192]{1,0:T(8,128)(2,1)S(1)} %collective-permute-done) | copy-start | bytes 3145732
  72.2 1.0 copy-start.8
  79.0 1.3 copy-start.2
  80.3 31.4 %copy-start.6 = (bf16[64,8192]{1,0:T(8,128)(2,1)}, bf16[64,8192]{1,0:T(8,128)(2,1)S(1)}, u32[]{:S(2)}) copy-start(bf16[64,8192]{1,0:T(8,128)(2,1)S(1)} %fusion.7) | copy-start | bytes 3145732
  113.2 162.0 %all-gather.5.cloned.1.call-start = ((), (), s32[]{:S(2)}) async-start(), calls=%async_computation.2 | async-start | bytes 4718592 | tf_op jit(solution)/shard_map/all_gather | solution.py:33
  114.0 39.5 %collective-permute-start.4 = (bf16[64,8192]{1,0:T(8,128)(2,1)}, bf16[64,8192]{1,0:T(8,128)(2,1)}, u32[]{:S(2)}, u32[]{:S(2)}) collective-permute-start(bf16[64,8192]{1,0:T(8,128)(2,1)} %get-tuple-element.24), channel_id=1, source_target_pairs={{8,0},{16,8},{24,16},{9,1},{17,9},{25,17},{10,2},{18,10},{26,18},{... | collective-permute-start | bytes 3145736 | tf_op jit(solution)/shard_map/ppermute | solution.py:23
  115.3 60.7 %collective-permute-start.5 = (bf16[64,8192]{1,0:T(8,128)(2,1)}, bf16[64,8192]{1,0:T(8,128)(2,1)}, u32[]{:S(2)}, u32[]{:S(2)}) collective-permute-start(bf16[64,8192]{1,0:T(8,128)(2,1)} %get-tuple-element.20), channel_id=1, source_target_pairs={{8,0},{16,8},{24,16},{9,1},{17,9},{25,17},{10,2},{18,10},{26,18},{... | collective-permute-start | bytes 3145736 | tf_op jit(solution)/shard_map/ppermute | solution.py:23
  116.8 80.1 %collective-permute-start.3 = (bf16[64,8192]{1,0:T(8,128)(2,1)}, bf16[64,8192]{1,0:T(8,128)(2,1)}, u32[]{:S(2)}, u32[]{:S(2)}) collective-permute-start(bf16[64,8192]{1,0:T(8,128)(2,1)} %copy-done.6), channel_id=1, source_target_pairs={{8,0},{16,8},{24,16},{9,1},{17,9},{25,17},{10,2},{18,10},{26,18},{... | collective-permute-start | bytes 3145736 | tf_op jit(solution)/shard_map/ppermute | solution.py:23
  154.9 22.5 %copy-start.3 = (f32[64,8192]{1,0:T(8,128)S(1)}, f32[64,8192]{1,0:T(8,128)}, u32[]{:S(2)}) copy-start(f32[64,8192]{1,0:T(8,128)} %copy-done.2) | copy-start | bytes 6291460
  181.3 6.7 %copy-start.5 = (f32[86,8192]{1,0:T(8,128)S(1)}, f32[86,8192]{1,0:T(8,128)}, u32[]{:S(2)}) copy-start(f32[86,8192]{1,0:T(8,128)} %get-tuple-element.29) | copy-start | bytes 8454148
  275.2 10.9 %copy-start.1 = (bf16[1024,256]{1,0:T(8,128)(2,1)S(1)}, bf16[1024,256]{1,0:T(8,128)(2,1)}, u32[]{:S(2)}) copy-start(bf16[1024,256]{1,0:T(8,128)(2,1)} %param.7) | copy-start | bytes 1572868
Sparse Core Ops, SparseCore 0:
  113.3 112.3 all-gather.2
  227.4 47.7 all-gather.4
where the time goes:
time: 293 us
  waiting for transfers between devices  175 us (60%)
  blocking collectives  31.3 us (11%)
  local copies, waits for them, and re-layouts  27.4 us (9%)
  matrix products  19 us (6%)
  other arithmetic  17 us (6%)
  between operations  14.9 us (5%)
  starting transfers between devices  8.58 us (3%)
    ppermute x3, waiting for transfers between devices, to_front(): return lax.ppermute(block, axis, [(i, i - 1) for i in range(1, n)])  60.5 us
    ppermute x3, waiting for transfers between devices, exchange(): return lax.ppermute(block, axis, [(i, partner(i, k, n)) for i in range(n)])  45 us
    all_gather x1, waiting for transfers between devices, body(): input_all = lax.all_gather(next_input, 'mp', axis=1, tiled=True)  42.9 us
    all_to_all x1, blocking collectives, body(): lax.all_to_all(new_weight, 'mp', split_axis=1, concat_axis=0, tiled=True)  31.3 us
    all_gather x1, waiting for transfers between devices, body(): weight_cols = lax.all_gather(weight_part, 'dp', axis=1, tiled=True)  25.5 us
    broadcast_in_dim x2, local copies, waits for them, and re-layouts, mine(): return lax.dynamic_slice_in_dim(rows, begin, shard_rows, 0)[None]  11.4 us
    dot_general x1, matrix products, body(): lax.dot_general(activations, out_grad, (((0,), (0,)), ((), ())), preferre...  10.7 us
    convert_element_type x3, other arithmetic, mine(): behind = to_front(block.astype(jnp.bfloat16), 'dp').astype(block.dtype)  8.57 us
  transfers between devices with their start and end apart: 8, of which 7 were waited for; matrix products, arithmetic and copies ran while one was open for 10% of the time, Pallas kernels for 0%

commit v1 on v0

--- a/solution.py
+++ b/solution.py
@@ -2,6 +2,18 @@
 import jax.numpy as jnp
 from jax import lax
 from jax.sharding import PartitionSpec as P
+
+
+def split_up(x, dim, count):
+    shape = x.shape
+    blocks = x.reshape(*shape[:dim], count, shape[dim] // count, *shape[dim + 1 :])
+    return jnp.moveaxis(blocks, dim, 0)
+
+
+def laid_out(blocks, dim):
+    blocks = jnp.moveaxis(blocks, 0, dim)
+    dims = blocks.shape
+    return blocks.reshape(*dims[:dim], dims[dim] * dims[dim + 1], *dims[dim + 2 :])
 
 
 def partner(i, k, n):
@@ -46,7 +58,16 @@
     new_second = 0.95 * old_second[0] + 0.05 * grad * grad
     update = new_first / first_fix / (jnp.sqrt(new_second / second_fix) + 1e-08)
     new_weight = (old_weight[0].astype(jnp.float32) - 0.01 * update).astype(jnp.bfloat16)
-    weight_part = lax.all_to_all(new_weight, "mp", split_axis=1, concat_axis=0, tiled=True)
+    size, mine_2 = (lax.axis_size("mp"), lax.axis_index("mp"))
+    blocks = split_up(new_weight, 1, size)
+    finished = [blocks[mine_2]]
+    for step_2 in range(1, size):
+        sent = blocks[(mine_2 + step_2) % size]
+        finished.append(
+            lax.ppermute(sent, "mp", [(i_2, (i_2 + step_2) % size) for i_2 in range(size)])
+        )
+    blocks = jnp.stack(finished)[(mine_2 - jnp.arange(size)) % size]
+    weight_part = laid_out(blocks, 0)
     heads = lax.axis_size("mp")
     weight_part = weight_part.reshape(heads, old_rows, -1)
     weight_cols = lax.all_gather(weight_part, "dp", axis=1, tiled=True)

time: 293 us -> 248 us (0.85)
  blocking collectives: 31.3 us -> 0 us
  waiting for transfers between devices: 175 us -> 146 us
  starting transfers between devices: 8.58 us -> 18.3 us
  local copies, waits for them, and re-layouts: 27.4 us -> 30.7 us
    all_gather x1, waiting for transfers between devices: 42.9 us -> 0.01 us  [body(): input_all = lax.all_gather(next_input, 'mp', axis=1, tiled=True)]
    all_to_all x1 -> x0, blocking collectives: 31.3 us -> none  [body(): lax.all_to_all(new_weight, 'mp', split_axis=1, concat_axis=0, tiled=True)]
    ppermute x0 -> x7, starting transfers between devices: none -> 9.81 us  [body(): lax.ppermute(sent, 'mp', [(i_2, (i_2 + step_2) % size) for i_2 in range(s...]
    all_gather x1, waiting for transfers between devices: 25.5 us -> 33.4 us  [body(): weight_cols = lax.all_gather(weight_part, 'dp', axis=1, tiled=True)]
    ppermute x0 -> x7, waiting for transfers between devices: none -> 6.67 us  [body(): lax.ppermute(sent, 'mp', [(i_2, (i_2 + step_2) % size) for i_2 in range(s...]
    all_gather x1 -> x0, local copies, waits for them, and re-layouts: 6.49 us -> none  [body(): weight_cols = lax.all_gather(weight_part, 'dp', axis=1, tiled=True)]
    unnamed x21 -> x34, local copies, waits for them, and re-layouts: 5.95 us -> 9.64 us
    another operation x1 -> x3, local copies, waits for them, and re-layouts: 0.01 us -> 2.95 us
  transfers between devices with their start and end apart: 8 -> 15, of which waited for: 7 -> 7; matrix products, arithmetic and copies ran while one was open for 10% -> 23% of each run, Pallas kernels for 0% -> 0%
where the time goes in v1:
time: 248 us
  waiting for transfers between devices  146 us (59%)
  local copies, waits for them, and re-layouts  30.7 us (12%)
  matrix products  20.2 us (8%)
  starting transfers between devices  18.3 us (7%)
  other arithmetic  17 us (7%)
  between operations  15 us (6%)
    ppermute x3, waiting for transfers between devices, to_front(): return lax.ppermute(block, axis, [(i, i - 1) for i in range(1, n)])  61 us
    ppermute x3, waiting for transfers between devices, exchange(): return lax.ppermute(block, axis, [(i, partner(i, k, n)) for i in range(n)])  44.5 us
    all_gather x1, waiting for transfers between devices, body(): weight_cols = lax.all_gather(weight_part, 'dp', axis=1, tiled=True)  33.4 us
    dot_general x1, matrix products, body(): lax.dot_general(activations, out_grad, (((0,), (0,)), ((), ())), preferre...  12.1 us
    broadcast_in_dim x2, local copies, waits for them, and re-layouts, mine(): return lax.dynamic_slice_in_dim(rows, begin, shard_rows, 0)[None]  11.4 us
    ppermute x7, starting transfers between devices, body(): lax.ppermute(sent, 'mp', [(i_2, (i_2 + step_2) % size) for i_2 in range(s...  9.81 us
    unnamed x34, local copies, waits for them, and re-layouts  9.64 us
    convert_element_type x3, other arithmetic, mine(): behind = to_front(block.astype(jnp.bfloat16), 'dp').astype(block.dtype)  8.57 us
  transfers between devices with their start and end apart: 15, of which 7 were waited for; matrix products, arithmetic and copies ran while one was open for 23% of the time, Pallas kernels for 0%

profile of v1, /device:TPU:0, one launch (start us, length us, event | category | flops | bytes accessed | tf_op | source)
XLA Modules:
  0.0 247.5 jit_solution(18103829863174968420)
XLA Ops:
  7.2 0.0 copy-start
  7.2 0.0 all-gather.4.cloned.1.call-start
  7.2 0.7 all-gather.4.cloned.1.call-update
  7.9 0.0 all-gather.6.cloned.1.call-start
  8.0 0.2 copy-done
  8.2 12.1 %convolution_convert_fusion = bf16[256,8192]{1,0:T(8,128)(2,1)} fusion(bf16[1024,256]{1,0:T(8,128)(2,1)S(1)} %copy-done, bf16[1024,8192]{1,0:T(8,128)(2,1)} %param.8), kind=kOutput, calls=%fused_computation.1 | convolution fusion | flops 4297064448 | bytes 21495808 | tf_op jit(solution)/shard_map/dot_general | solution.py:46
  20.3 3.7 %dynamic-slice_bitcast_fusion.2 = (bf16[64,8192]{1,0:T(8,128)(2,1)}, bf16[64,8192]{1,0:T(8,128)(2,1)}, bf16[64,8192]{1,0:T(8,128)(2,1)}) fusion(bf16[4,64,8192]{2,1,0:T(8,128)(2,1)} %bitcast.77, s32[]{:T(128)S(6)} %select_n.97, s32[]{:T(128)S(6)} %select_n.99, s32[]{:T(128)S(6)} %select_n.98), kind=kLoop, calls=%fused_computation.26 | loop fusion | bytes 6291468 | tf_op jit(solution)/shard_map/jit(dynamic_index_in_dim)/squeeze | solution.py:52
  24.1 3.8 %collective-permute-start.2 = (bf16[64,8192]{1,0:T(8,128)(2,1)}, bf16[64,8192]{1,0:T(8,128)(2,1)S(1)}, u32[]{:S(2)}, u32[]{:S(2)}) collective-permute-start(bf16[64,8192]{1,0:T(8,128)(2,1)} %get-tuple-element.23), channel_id=1, source_target_pairs={{0,24},{8,16},{16,8},{24,0},{1,25},{9,17},{17,9},{25,1},{2,26},{10... | collective-permute-start | bytes 3145736 | tf_op jit(solution)/shard_map/ppermute | solution.py:25
  27.9 0.5 collective-permute-start.1
  28.4 0.1 collective-permute-start
  29.2 0.0 copy-start.8
  29.3 22.9 %collective-permute-done.2 = bf16[64,8192]{1,0:T(8,128)(2,1)S(1)} collective-permute-done((bf16[64,8192]{1,0:T(8,128)(2,1)}, bf16[64,8192]{1,0:T(8,128)(2,1)S(1)}, u32[]{:S(2)}, u32[]{:S(2)}) %collective-permute-start.2) | collective-permute-done | bytes 1048608 | tf_op jit(solution)/shard_map/ppermute | solution.py:25
  52.1 21.6 %collective-permute-done.1 = bf16[64,8192]{1,0:T(8,128)(2,1)S(1)} collective-permute-done((bf16[64,8192]{1,0:T(8,128)(2,1)}, bf16[64,8192]{1,0:T(8,128)(2,1)S(1)}, u32[]{:S(2)}, u32[]{:S(2)}) %collective-permute-start.1) | collective-permute-done | bytes 1048608 | tf_op jit(solution)/shard_map/ppermute | solution.py:25
  73.7 0.0 copy-done.6
  73.7 1.0 copy-done.7
  74.7 0.0 collective-permute-done
  74.7 5.9 %fusion.13 = (bf16[64,8192]{1,0:T(8,128)(2,1)}, f32[64,8192]{1,0:T(8,128)S(1)}, bf16[64,8192]{1,0:T(8,128)(2,1)}, f32[64,8192]{1,0:T(8,128)S(1)}) fusion(bf16[64,8192]{1,0:T(8,128)(2,1)} %copy-done.6, bf16[64,8192]{1,0:T(8,128)(2,1)} %copy-done.7, bf16[64,8192]{1,0:T(8,128)(2,1)} %collective-permute-done, bf16[4,64,8192]{2,1,0:T(8,128)(2,1)} %bitcast.78, ...), kind=kLoop, calls=%fused_computation.59 | loop fusion | flops 8388608 | bytes 14680068 | tf_op jit(solution)/shard_map/convert_element_type | solution.py:78
  80.6 0.0 copy-done.8
  80.6 1.1 fusion.7
  81.6 0.2 copy-done.2
  81.9 0.6 copy.22
  82.5 2.3 constant_dynamic-slice_fusion
  84.8 0.2 collective-permute-start.6
  85.0 1.8 collective-permute-start.7
  86.9 2.5 %collective-permute-start.8 = (bf16[64,1024]{1,0:T(8,128)(2,1)S(1)}, bf16[64,1024]{1,0:T(8,128)(2,1)S(1)}, u32[]{:S(2)}, u32[]{:S(2)}) collective-permute-start(bf16[64,1024]{1,0:T(8,128)(2,1)S(1)} %bitcast.85), channel_id=1, source_target_pairs={{0,3},{1,4},{2,5},{3,6},{4,7},{5,0},{6,1},{7,2},{8,11},{9,12},{10,... | collective-permute-start | bytes 393224 | tf_op jit(solution)/shard_map/ppermute | solution.py:67
  89.5 1.3 collective-permute-start.9
  90.8 1.3 collective-permute-start.10
  92.2 0.7 bitcast_dynamic-update-slice_fusion
  92.9 0.0 collective-permute-done.6
  92.9 1.3 collective-permute-start.11
  94.3 0.7 bitcast_dynamic-update-slice_fusion.7
  94.9 0.0 collective-permute-done.7
  95.0 1.3 collective-permute-start.12
  96.3 0.7 bitcast_dynamic-update-slice_fusion.6
  97.0 6.7 %collective-permute-done.8 = bf16[64,1024]{1,0:T(8,128)(2,1)S(1)} collective-permute-done((bf16[64,1024]{1,0:T(8,128)(2,1)S(1)}, bf16[64,1024]{1,0:T(8,128)(2,1)S(1)}, u32[]{:S(2)}, u32[]{:S(2)}) %collective-permute-start.8) | collective-permute-done | bytes 131104 | tf_op jit(solution)/shard_map/ppermute | solution.py:67
  103.6 0.7 bitcast_dynamic-update-slice_fusion.5
  104.3 0.0 collective-permute-done.9
  104.3 0.7 bitcast_dynamic-update-slice_fusion.4
  104.9 0.0 collective-permute-done.10
  104.9 0.7 bitcast_dynamic-update-slice_fusion.3
  105.6 0.0 collective-permute-done.11
  105.6 0.7 bitcast_dynamic-update-slice_fusion.2
  106.3 0.0 collective-permute-done.12
  106.3 0.7 bitcast_dynamic-update-slice_fusion.1
  106.9 2.8 %gather_fusion = bf16[8,64,1024]{2,1,0:T(8,128)(2,1)} fusion(bf16[8,64,1024]{2,1,0:T(8,128)(2,1)} %bitcast_dynamic-update-slice_fusion.1, s32[1024]{0:T(1024)S(1)} %pad_clamp_fusion), kind=kCustom, calls=%fused_computation | custom fusion | bytes 2097184 | tf_op jit(solution)/shard_map/gather | solution.py:69
  109.8 0.0 all-gather.6.cloned.1.call-update
  109.8 1.3 collective-permute-start.5
  111.1 1.3 collective-permute-start.4
  112.4 0.1 pad_dynamic-slice_fusion.7
  112.5 0.1 pad_dynamic-slice_fusion.6
  112.6 1.5 collective-permute-start.3
  114.0 33.9 %collective-permute-done.5 = bf16[64,8192]{1,0:T(8,128)(2,1)} collective-permute-done((bf16[64,8192]{1,0:T(8,128)(2,1)}, bf16[64,8192]{1,0:T(8,128)(2,1)}, u32[]{:S(2)}, u32[]{:S(2)}) %collective-permute-start.5) | collective-permute-done | bytes 1048608 | tf_op jit(solution)/shard_map/ppermute | solution.py:35
  147.9 1.4 convert_element_type.62
  149.3 0.0 copy-start.3
  149.3 21.4 %collective-permute-done.4 = bf16[64,8192]{1,0:T(8,128)(2,1)} collective-permute-done((bf16[64,8192]{1,0:T(8,128)(2,1)}, bf16[64,8192]{1,0:T(8,128)(2,1)}, u32[]{:S(2)}, u32[]{:S(2)}) %collective-permute-start.4) | collective-permute-done | bytes 1048608 | tf_op jit(solution)/shard_map/ppermute | solution.py:35
  170.8 1.4 convert_element_type.60
  172.1 4.0 %fusion.1 = (f32[86,8192]{1,0:T(8,128)}, f32[86,8192]{1,0:T(8,128)}) fusion(s32[]{:T(128)S(6)} %select_n.100, f32[64,8192]{1,0:T(8,128)S(1)} %get-tuple-element.17, f32[64,8192]{1,0:T(8,128)S(1)} %convert_element_type.62, f32[86]{0:T(128)S(1)} %pad_dynamic-slice_fusion.6, f32[64,8192]{1,0:T(8,128)S(1)} %convert_element_type.60, f32[64,8192]{1,0:T(8,128)S(1)} %copy-done.3), kind=kLoop, calls=%fused_computation.10 | loop fusion | flops 2818048 | bytes 14025052 | tf_op jit(solution)/shard_map/concatenate | solution.py:79
  176.1 6.7 %broadcast_in_dim.15 = f32[1,86,8192]{2,0,1:T(1,128)} reshape(f32[86,8192]{1,0:T(8,128)} %get-tuple-element.34) | data formatting | bytes 5636096 | tf_op jit(solution)/shard_map/broadcast_in_dim | solution.py:80
  182.8 4.7 %broadcast_in_dim.16 = f32[1,86,8192]{2,0,1:T(1,128)} reshape(f32[86,8192]{1,0:T(8,128)S(1)} %copy-done.4) | data formatting | bytes 5636096 | tf_op jit(solution)/shard_map/broadcast_in_dim | solution.py:80
  187.5 5.7 %collective-permute-done.3 = bf16[64,8192]{1,0:T(8,128)(2,1)} collective-permute-done((bf16[64,8192]{1,0:T(8,128)(2,1)}, bf16[64,8192]{1,0:T(8,128)(2,1)}, u32[]{:S(2)}, u32[]{:S(2)}) %collective-permute-start.3) | collective-permute-done | bytes 1048608 | tf_op jit(solution)/shard_map/ppermute | solution.py:35
  193.2 3.4 %fusion.10 = bf16[1,86,8192]{2,1,0:T(8,128)(2,1)} fusion(s32[]{:T(128)S(6)} %select_n.100, bf16[64,8192]{1,0:T(8,128)(2,1)} %copy-done.5, bf16[64,8192]{1,0:T(8,128)(2,1)} %collective-permute-done.3, bf16[86]{0:T(256)(128)(2,1)S(1)} %pad_dynamic-slice_fusion.7), kind=kLoop, calls=%fused_computation.23 | loop fusion | flops 4227072 | bytes 3506352 | tf_op jit(solution)/shard_map/broadcast_in_dim | solution.py:80
  196.6 33.4 %all-gather.6.cloned.1.call-done = bf16[8,256,1024]{2,1,0:T(8,128)(2,1)} async-done(((bf16[8,64,1024]{2,1,0:T(8,128)(2,1)}), bf16[8,256,1024]{2,1,0:T(8,128)(2,1)}) %all-gather.6.cloned.1.call-update) | async-done | bytes 4194320 | tf_op jit(solution)/shard_map/all_gather | solution.py:73
  230.0 8.0 %convert_bitcast_fusion = bf16[1024,1024]{0,1:T(8,128)(2,1)S(1)} fusion(bf16[2048,1024]{1,0:T(8,128)(2,1)} %bitcast.88, bf16[1024,2048]{1,0:T(8,128)(2,1)} %all-gather.4.cloned.1.call-done), kind=kOutput, calls=%fused_computation.20 | convolution fusion | flops 4296015872 | bytes 10485760 | tf_op jit(solution)/shard_map/dot_general | solution.py:83
  238.1 2.6 %copy.13 = bf16[1024,1024]{1,0:T(8,128)(2,1)} copy(bf16[1024,1024]{0,1:T(8,128)(2,1)S(1)} %convert_bitcast_fusion) | data formatting | bytes 4194304
  (22 shorter events, 0.4 us)
Async XLA Ops:
  7.2 1.1 copy-start
  7.2 189.4 %all-gather.4.cloned.1.call-start = ((), (), s32[]{:S(2)}) async-start(), calls=%async_computation | async-start | bytes 4718592 | tf_op jit(solution)/shard_map/all_gather | solution.py:45
  7.9 222.1 %all-gather.6.cloned.1.call-start = ((), (), s32[]{:S(2)}) async-start(), calls=%async_computation.1 | async-start | bytes 5242880 | tf_op jit(solution)/shard_map/all_gather | solution.py:73
  24.1 28.1 %collective-permute-start.2 = (bf16[64,8192]{1,0:T(8,128)(2,1)}, bf16[64,8192]{1,0:T(8,128)(2,1)S(1)}, u32[]{:S(2)}, u32[]{:S(2)}) collective-permute-start(bf16[64,8192]{1,0:T(8,128)(2,1)} %get-tuple-element.23), channel_id=1, source_target_pairs={{0,24},{8,16},{16,8},{24,0},{1,25},{9,17},{17,9},{25,1},{2,26},{10... | collective-permute-start | bytes 3145736 | tf_op jit(solution)/shard_map/ppermute | solution.py:25
  27.9 45.8 %collective-permute-start.1 = (bf16[64,8192]{1,0:T(8,128)(2,1)}, bf16[64,8192]{1,0:T(8,128)(2,1)S(1)}, u32[]{:S(2)}, u32[]{:S(2)}) collective-permute-start(bf16[64,8192]{1,0:T(8,128)(2,1)} %get-tuple-element.24), channel_id=1, source_target_pairs={{0,16},{8,24},{16,0},{24,8},{1,17},{9,25},{17,1},{25,9},{2,18},{10... | collective-permute-start | bytes 3145736 | tf_op jit(solution)/shard_map/ppermute | solution.py:25
  28.4 46.3 %collective-permute-start = (bf16[64,8192]{1,0:T(8,128)(2,1)}, bf16[64,8192]{1,0:T(8,128)(2,1)}, u32[]{:S(2)}, u32[]{:S(2)}) collective-permute-start(bf16[64,8192]{1,0:T(8,128)(2,1)} %get-tuple-element.22), channel_id=1, source_target_pairs={{0,8},{8,0},{16,24},{24,16},{1,9},{9,1},{17,25},{25,17},{2,10},{10... | collective-permute-start | bytes 3145736 | tf_op jit(solution)/shard_map/ppermute | solution.py:25
  29.2 51.3 %copy-start.8 = (bf16[1,64,8192]{2,1,0:T(8,128)(2,1)S(1)}, bf16[1,64,8192]{2,1,0:T(8,128)(2,1)}, u32[]{:S(2)}) copy-start(bf16[1,64,8192]{2,1,0:T(8,128)(2,1)} %param.9) | copy-start | bytes 3145732
  52.1 21.6 %copy-start.6 = (bf16[64,8192]{1,0:T(8,128)(2,1)}, bf16[64,8192]{1,0:T(8,128)(2,1)S(1)}, u32[]{:S(2)}) copy-start(bf16[64,8192]{1,0:T(8,128)(2,1)S(1)} %collective-permute-done.2) | copy-start | bytes 3145732
  73.7 1.0 copy-start.7
  80.6 1.3 copy-start.2
  81.9 2.9 %copy-start.5 = (bf16[64,8192]{1,0:T(8,128)(2,1)}, bf16[64,8192]{1,0:T(8,128)(2,1)S(1)}, u32[]{:S(2)}) copy-start(bf16[64,8192]{1,0:T(8,128)(2,1)S(1)} %fusion.7) | copy-start | bytes 3145732
  84.8 8.1 %collective-permute-start.6 = (bf16[64,1024]{1,0:T(8,128)(2,1)S(1)}, bf16[64,1024]{1,0:T(8,128)(2,1)S(1)}, u32[]{:S(2)}, u32[]{:S(2)}) collective-permute-start(bf16[64,1024]{1,0:T(8,128)(2,1)S(1)} %bitcast.87), channel_id=1, source_target_pairs={{0,1},{1,2},{2,3},{3,4},{4,5},{5,6},{6,7},{7,0},{8,9},{9,10},{10,1... | collective-permute-start | bytes 393224 | tf_op jit(solution)/shard_map/ppermute | solution.py:67
  85.0 9.9 %collective-permute-start.7 = (bf16[64,1024]{1,0:T(8,128)(2,1)S(1)}, bf16[64,1024]{1,0:T(8,128)(2,1)S(1)}, u32[]{:S(2)}, u32[]{:S(2)}) collective-permute-start(bf16[64,1024]{1,0:T(8,128)(2,1)S(1)} %bitcast.86), channel_id=1, source_target_pairs={{0,2},{1,3},{2,4},{3,5},{4,6},{5,7},{6,0},{7,1},{8,10},{9,11},{10,... | collective-permute-start | bytes 393224 | tf_op jit(solution)/shard_map/ppermute | solution.py:67
  86.9 16.7 %collective-permute-start.8 = (bf16[64,1024]{1,0:T(8,128)(2,1)S(1)}, bf16[64,1024]{1,0:T(8,128)(2,1)S(1)}, u32[]{:S(2)}, u32[]{:S(2)}) collective-permute-start(bf16[64,1024]{1,0:T(8,128)(2,1)S(1)} %bitcast.85), channel_id=1, source_target_pairs={{0,3},{1,4},{2,5},{3,6},{4,7},{5,0},{6,1},{7,2},{8,11},{9,12},{10,... | collective-permute-start | bytes 393224 | tf_op jit(solution)/shard_map/ppermute | solution.py:67
  89.5 14.8 %collective-permute-start.9 = (bf16[64,1024]{1,0:T(8,128)(2,1)S(1)}, bf16[64,1024]{1,0:T(8,128)(2,1)S(1)}, u32[]{:S(2)}, u32[]{:S(2)}) collective-permute-start(bf16[64,1024]{1,0:T(8,128)(2,1)S(1)} %bitcast.84), channel_id=1, source_target_pairs={{0,4},{1,5},{2,6},{3,7},{4,0},{5,1},{6,2},{7,3},{8,12},{9,13},{10,... | collective-permute-start | bytes 393224 | tf_op jit(solution)/shard_map/ppermute | solution.py:67
  90.8 14.1 %collective-permute-start.10 = (bf16[64,1024]{1,0:T(8,128)(2,1)S(1)}, bf16[64,1024]{1,0:T(8,128)(2,1)S(1)}, u32[]{:S(2)}, u32[]{:S(2)}) collective-permute-start(bf16[64,1024]{1,0:T(8,128)(2,1)S(1)} %bitcast.83), channel_id=1, source_target_pairs={{0,5},{1,6},{2,7},{3,0},{4,1},{5,2},{6,3},{7,4},{8,13},{9,14},{10,... | collective-permute-start | bytes 393224 | tf_op jit(solution)/shard_map/ppermute | solution.py:67
  92.9 12.7 %collective-permute-start.11 = (bf16[64,1024]{1,0:T(8,128)(2,1)S(1)}, bf16[64,1024]{1,0:T(8,128)(2,1)S(1)}, u32[]{:S(2)}, u32[]{:S(2)}) collective-permute-start(bf16[64,1024]{1,0:T(8,128)(2,1)S(1)} %bitcast.82), channel_id=1, source_target_pairs={{0,6},{1,7},{2,0},{3,1},{4,2},{5,3},{6,4},{7,5},{8,14},{9,15},{10,... | collective-permute-start | bytes 393224 | tf_op jit(solution)/shard_map/ppermute | solution.py:67
  95.0 11.3 %collective-permute-start.12 = (bf16[64,1024]{1,0:T(8,128)(2,1)S(1)}, bf16[64,1024]{1,0:T(8,128)(2,1)S(1)}, u32[]{:S(2)}, u32[]{:S(2)}) collective-permute-start(bf16[64,1024]{1,0:T(8,128)(2,1)S(1)} %bitcast.81), channel_id=1, source_target_pairs={{0,7},{1,0},{2,1},{3,2},{4,3},{5,4},{6,5},{7,6},{8,15},{9,8},{10,9... | collective-permute-start | bytes 393224 | tf_op jit(solution)/shard_map/ppermute | solution.py:67
  109.8 38.2 %collective-permute-start.5 = (bf16[64,8192]{1,0:T(8,128)(2,1)}, bf16[64,8192]{1,0:T(8,128)(2,1)}, u32[]{:S(2)}, u32[]{:S(2)}) collective-permute-start(bf16[64,8192]{1,0:T(8,128)(2,1)} %get-tuple-element.16), channel_id=1, source_target_pairs={{8,0},{16,8},{24,16},{9,1},{17,9},{25,17},{10,2},{18,10},{26,18},{... | collective-permute-start | bytes 3145736 | tf_op jit(solution)/shard_map/ppermute | solution.py:35
  111.1 59.7 %collective-permute-start.4 = (bf16[64,8192]{1,0:T(8,128)(2,1)}, bf16[64,8192]{1,0:T(8,128)(2,1)}, u32[]{:S(2)}, u32[]{:S(2)}) collective-permute-start(bf16[64,8192]{1,0:T(8,128)(2,1)} %get-tuple-element.20), channel_id=1, source_target_pairs={{8,0},{16,8},{24,16},{9,1},{17,9},{25,17},{10,2},{18,10},{26,18},{... | collective-permute-start | bytes 3145736 | tf_op jit(solution)/shard_map/ppermute | solution.py:35
  112.6 80.7 %collective-permute-start.3 = (bf16[64,8192]{1,0:T(8,128)(2,1)}, bf16[64,8192]{1,0:T(8,128)(2,1)}, u32[]{:S(2)}, u32[]{:S(2)}) collective-permute-start(bf16[64,8192]{1,0:T(8,128)(2,1)} %copy-done.5), channel_id=1, source_target_pairs={{8,0},{16,8},{24,16},{9,1},{17,9},{25,17},{10,2},{18,10},{26,18},{... | collective-permute-start | bytes 3145736 | tf_op jit(solution)/shard_map/ppermute | solution.py:35
  149.3 22.8 %copy-start.3 = (f32[64,8192]{1,0:T(8,128)S(1)}, f32[64,8192]{1,0:T(8,128)}, u32[]{:S(2)}) copy-start(f32[64,8192]{1,0:T(8,128)} %copy-done.2) | copy-start | bytes 6291460
  176.1 6.7 %copy-start.4 = (f32[86,8192]{1,0:T(8,128)S(1)}, f32[86,8192]{1,0:T(8,128)}, u32[]{:S(2)}) copy-start(f32[86,8192]{1,0:T(8,128)} %get-tuple-element.33) | copy-start | bytes 8454148
  230.0 10.6 %copy-start.1 = (bf16[1024,256]{1,0:T(8,128)(2,1)S(1)}, bf16[1024,256]{1,0:T(8,128)(2,1)}, u32[]{:S(2)}) copy-start(bf16[1024,256]{1,0:T(8,128)(2,1)} %param.7) | copy-start | bytes 1572868
Sparse Core Ops, SparseCore 0:
  9.6 50.4 all-gather.3
  109.9 120.0 all-gather.5
